TPU v7x, 512 devices: a whole 4x4x16 slice. The times are simulated.
512 devices in a mesh: row: 4 (over x), col: 16 (over y, z_hi, core), ch: 8 (over z_lo).
Axes of the slice: x: 4, y: 4, z: 16 (z_hi: 2, z_lo: 8; z = z_hi * 8 + z_lo), core: 2. Of those that a mesh axis runs over, the one named last changes fastest.
Arguments:
- pair: bfloat16 [512, 512, 128], P('col', 'row'), may hold values from -6 to 6
- token_mask: int32 [512], replicated, may hold values 0 or 1
- pair_mask: int32 [512, 512], P('col', 'row'), may hold values 0 or 1
- ln_gain: float32 [128], replicated, may hold values from 0.5 to 1.5
- w_in: bfloat16 [128, 4, 128], P(None, None, 'ch'), may hold values from -0.5 to 0.5
- grad_tri: bfloat16 [128, 512, 512], P('ch', 'col'), may hold values from -0.29882812 to 0.29882812
Outputs:
- d_pair: bfloat16 [512, 512, 128], P('col', 'row')
- w_grad: float32 [128, 4, 128], P(None, None, 'ch')
All inputs are finite; a program needn't handle non-finite values. No bound on the sum of `pair_mask` on one device may be relied on, other than what follows from the above.
Results may differ from a plain program's by a relative error of at most 0.012.
Values may be sent and summed in bfloat16 or wider, within the bound.
A program may use at most 64 MiB of HBM per device.

v0:
```python
import jax
import jax.numpy as jnp
from jax import lax
from jax.sharding import PartitionSpec as P

EPS = 1e-05


def layer_stats(pair, ln_gain):
    values = pair.astype(jnp.float32)
    mean_val = jnp.mean(values, axis=-1, keepdims=True)
    centred = values - mean_val
    inv_std = lax.rsqrt(jnp.mean(centred * centred, axis=-1, keepdims=True) + EPS)
    standard = centred * inv_std
    normed = (standard * ln_gain).astype(jnp.bfloat16)
    return (standard, inv_std, normed)


def gated(proj, masking):
    sig_left = jax.nn.sigmoid(proj[1])
    sig_right = jax.nn.sigmoid(proj[3])
    left = (masking * sig_left * proj[0]).astype(jnp.bfloat16)
    right = (masking * sig_right * proj[2]).astype(jnp.bfloat16)
    return (left, right, sig_left, sig_right)


def input_grads(proj, masking, sig_left, sig_right, d_left, d_right):
    grad_l = d_left.astype(jnp.float32) * masking
    grad_r = d_right.astype(jnp.float32) * masking
    stacked = jnp.stack(
        [
            grad_l * sig_left,
            grad_l * proj[0] * sig_left * (1.0 - sig_left),
            grad_r * sig_right,
            grad_r * proj[2] * sig_right * (1.0 - sig_right),
        ]
    )
    return stacked.astype(jnp.bfloat16)


def norm_back(d_norm, standard, inv_std, ln_gain):
    scaled = d_norm * ln_gain
    first = jnp.mean(scaled, axis=-1, keepdims=True)
    second = jnp.mean(scaled * standard, axis=-1, keepdims=True)
    return (inv_std * (scaled - first - standard * second)).astype(jnp.bfloat16)


def body(pair, token_mask, pair_mask, ln_gain, w_in, grad_tri):
    rows_i = pair.shape[0]
    rows_k = pair.shape[1]
    full_n = token_mask.shape[0]
    first_start = lax.axis_index("col") * rows_i
    second_start = lax.axis_index("row") * rows_k
    tok_first = lax.dynamic_slice_in_dim(token_mask, first_start, rows_i, 0).astype(jnp.float32)
    tok_second = lax.dynamic_slice_in_dim(token_mask, second_start, rows_k, 0).astype(jnp.float32)
    masking = pair_mask.astype(jnp.float32) * tok_first[:, None] * tok_second[None, :]
    standard, inv_std, normed = layer_stats(pair, ln_gain)
    proj = jnp.einsum("ikc,cgh->ghik", normed, w_in, preferred_element_type=jnp.float32)
    left, right, sig_left, sig_right = gated(proj, masking)
    grad_part = grad_tri
    d_left = jnp.einsum(
        "hij,hjk->hik",
        grad_part,
        lax.all_gather(right, "col", axis=1, tiled=True),
        preferred_element_type=jnp.float32,
    )
    grad_part = grad_tri
    summed = lax.psum_scatter(
        jnp.einsum("hij,hik->jhk", grad_part, left, preferred_element_type=jnp.float32),
        "col",
        scatter_dimension=0,
        tiled=True,
    )
    d_right = jnp.transpose(summed, (1, 0, 2))
    d_left = d_left.astype(jnp.bfloat16)
    d_right = d_right.astype(jnp.bfloat16)
    grads = input_grads(proj, masking, sig_left, sig_right, d_left, d_right)
    norm_part = jnp.einsum("ghik,cgh->ikc", grads, w_in, preferred_element_type=jnp.float32)
    d_norm = lax.psum(norm_part, "ch")
    weight_part = jnp.einsum("ikc,ghik->cgh", normed, grads, preferred_element_type=jnp.float32)
    w_grad = lax.psum(weight_part, ("row", "col")) / full_n
    d_pair = norm_back(d_norm, standard, inv_std, ln_gain)
    return (d_pair, w_grad)


def solution(mesh):
    return jax.shard_map(
        body,
        mesh=mesh,
        in_specs=(
            P("col", "row", None),
            P(),
            P("col", "row"),
            P(),
            P(None, None, "ch"),
            P("ch", "col", None),
        ),
        out_specs=(P("col", "row", None), P(None, None, "ch")),
        check_vma=False,
    )
```

profile of v0, /device:TPU:1, one launch (start us, length us, event | category | flops | bytes accessed | tf_op | source)
XLA Modules:
  0.0 827.1 jit_solution(13798723192781740617)
XLA Ops:
  7.2 0.0 copy-start
  7.2 0.0 copy-start.1
  7.2 0.0 copy-start.3
  7.2 0.0 copy-start.4
  7.2 0.0 copy-start.5
  7.2 0.0 all-gather.2.cloned.1.call-start
  7.3 0.9 dynamic-slice_convert_fusion
  8.1 0.8 dynamic-slice_convert_fusion.1
  8.9 1.6 convert_reduce_fusion
  10.5 2.3 fusion.10
  12.8 0.0 copy-done.3
  12.8 0.1 multiply_multiply_fusion
  12.9 0.0 copy-done.1
  12.9 0.0 copy-done.4
  12.9 0.0 copy-done.5
  12.9 1.3 convolution_bitcast_fusion.1
  14.3 0.7 multiply_convert_fusion.1
  15.0 0.0 all-gather.2.cloned.1.call-update
  15.0 0.0 reduce-scatter.2.cloned.1.call-start
  15.1 98.0 %all-gather.2.cloned.1.call-done = bf16[16,512,128]{2,0,1:T(8,128)(2,1)} async-done(((bf16[16,32,128]{2,0,1:T(8,128)(2,1)}), bf16[16,512,128]{2,0,1:T(8,128)(2,1)}) %all-gather.2.cloned.1.call-update) | async-done | bytes 2097168 | tf_op jit(solution)/shard_map/all_gather | solution.py:64
  113.1 0.0 copy-done
  113.1 2.4 fusion.11
  115.5 0.2 fusion.38
  115.7 2.7 fusion.41
  118.4 5.4 copy.22
  123.8 0.0 reduce-scatter.2.cloned.1.call-update
  123.8 0.0 all-reduce.2.cloned.1.call-start
  123.9 142.8 %reduce-scatter.2.cloned.1.call-done = f32[32,16,128]{2,1,0:T(8,128)} async-done(((f32[512,16,128]{2,1,0:T(8,128)}), f32[32,16,128]{2,1,0:T(8,128)}) %reduce-scatter.2.cloned.1.call-update) | async-done | bytes 262160 | tf_op jit(solution)/shard_map/reduce_scatter | solution.py:68
  266.7 1.1 fusion.40
  267.8 1.8 convolution_bitcast_fusion
  269.6 0.0 all-reduce.2.cloned.1.call-update
  269.6 1.3 convolution_bitcast_fusion.2
  270.9 541.7 %psum.15 = f32[128,4,16]{0,2,1:T(8,128)S(1)} all-reduce(f32[128,4,16]{0,2,1:T(8,128)S(1)} %convolution_bitcast_fusion.2), channel_id=1, replica_groups=mesh['row'=4,'col'=16,'ch'=8] {'row','col'}, use_global_device_ids=true, to_apply=%region_6.0 | all-reduce | flops 8192 | bytes 65536 | tf_op jit(solution)/shard_map/psum | solution.py:81
  812.6 0.6 broadcast_multiply_fusion
  813.2 0.0 all-reduce.2.cloned.1.call-done
  813.2 0.0 copy-start.2
  813.2 4.1 multiply_reduce_fusion
  817.3 0.0 copy-done.2
  817.3 3.3 fusion.9
  (3 shorter events, 0.0 us)
Async XLA Ops:
  7.2 106.0 %copy-start = (bf16[16,32,512]{2,1,0:T(8,128)(2,1)S(1)}, bf16[16,32,512]{2,1,0:T(8,128)(2,1)}, u32[]{:S(2)}) copy-start(bf16[16,32,512]{2,1,0:T(8,128)(2,1)} %param.11) | copy-start | bytes 1572868
  7.2 5.7 copy-start.1
  7.2 5.6 copy-start.3
  7.2 5.7 copy-start.4
  7.2 5.7 copy-start.5
  7.2 105.9 %all-gather.2.cloned.1.call-start = ((), (), s32[]{:S(2)}) async-start(), calls=%async_computation.1 | async-start | bytes 2228224 | tf_op jit(solution)/shard_map/all_gather | solution.py:64
  15.0 251.7 %reduce-scatter.2.cloned.1.call-start = ((), (), s32[]{:S(2)}) async-start(), calls=%async_computation.2 | async-start | bytes 4456448 | tf_op jit(solution)/shard_map/reduce_scatter | solution.py:68
  123.8 689.4 %all-reduce.2.cloned.1.call-start = ((), (), s32[]{:S(2)}) async-start(), calls=%async_computation.3 | async-start | bytes 4194304 | tf_op jit(solution)/shard_map/psum | solution.py:79
  813.2 4.1 copy-start.2
Sparse Core Ops, SparseCore 0:
  15.2 97.9 all-gather.1
  124.0 142.6 reduce-scatter.1
  269.9 130.0 all-reduce.1
where the time goes:
time: 843 us; the launch traced here: 827 us
  blocking collectives  542 us (64%)
  waiting for transfers between devices  241 us (29%)
  other arithmetic  15.5 us (2%)
  between operations  13.9 us (2%)
  matrix products  9.49 us (1%)
    psum x1, blocking collectives, body(): w_grad = lax.psum(weight_part, ('row', 'col')) / full_n  542 us
    reduce_scatter x1, waiting for transfers between devices, body(): lax.psum_scatter(jnp.einsum('hij,hik->jhk', grad_part, left, preferred_el...  143 us
    all_gather x1, waiting for transfers between devices, body(): lax.all_gather(right, 'col', axis=1, tiled=True)  98 us
  transfers between devices with their start and end apart: 3, of which 2 were waited for; matrix products, arithmetic and copies ran while one was open for 0% of the time, Pallas kernels for 0%

commit v1 on v0

v1 whole, which is shorter than its diff:
```python
import functools

import jax
import jax.numpy as jnp
from jax import lax
from jax.experimental import pallas as pl
from jax.experimental.pallas import tpu as pltpu
from jax.sharding import PartitionSpec as P

EPS = 1e-05
F32 = jnp.float32
BF16 = jnp.bfloat16
MESH = pl.DeviceIdType.MESH
NT = (((1,), (1,)), ((), ()))
TN = (((0,), (0,)), ((), ()))


def normalise(x):
    mean = jnp.mean(x, axis=-1, keepdims=True)
    cen = x - mean
    inv = lax.rsqrt(jnp.mean(cen * cen, axis=-1, keepdims=True) + EPS)
    return cen * inv, inv


def factors(p, m):
    p0, p1, p2, p3 = p
    s1 = jax.nn.sigmoid(p1)
    s3 = jax.nn.sigmoid(p3)
    f0 = m * s1
    f2 = m * s3
    left = f0 * p0
    right = f2 * p2
    return (f0, left * (1.0 - s1), f2, right * (1.0 - s3)), left, right


def kernel(
    nr, nc, nq,
    tok_s, tok_v, pair, pm, gain, wt, gt,
    out, wout,
    normed, fac, lt, rt, lrs, lrr, gfull, dsend, drecv, df, asend, arecv,
    wf, fo, stdo, invo, ag, ws, wr, xr, wg,
    g1_s, g1_r, g2_s, g2_r, wf_s, wf_r, lr_s, lr_r, d_s, d_r, a_s, a_r,
    ag_s, ag_r, wa_s, wa_r, wb_s, wb_r, wc_s, wc_r,
):
    r = lax.axis_index("row")
    c = lax.axis_index("col")
    q = lax.axis_index("ch")
    ni, nk, cc = pair.shape
    hq = wt.shape[0] // 4
    n = nc * ni
    nj = gfull.shape[2]
    t_n = ni // nq
    jpb = nj // ni

    def peer(axis, size, me, off):
        return lax.rem(me + off, size)

    def remote(src, dst, s, rr, axis, to):
        return pltpu.make_async_remote_copy(
            src_ref=src, dst_ref=dst, send_sem=s, recv_sem=rr,
            device_id={axis: to}, device_id_type=MESH,
        )

    barrier = pltpu.get_barrier_semaphore()
    for axis, size, me in (("row", nr, r), ("col", nc, c), ("ch", nq, q)):
        def greet(off, carry, axis=axis, size=size, me=me):
            pl.semaphore_signal(
                barrier, inc=1, device_id={axis: peer(axis, size, me, off)},
                device_id_type=MESH,
            )
            return carry
        lax.fori_loop(1, size, greet, 0)
    pl.semaphore_wait(barrier, nr + nc + nq - 3)

    def spread(size, me, make, start=True):
        def one(off, carry):
            to = lax.rem(me + off, size)
            copy = make(to, to, me)
            if start:
                copy.start()
            else:
                copy.wait_send()
            return carry
        lax.fori_loop(1, size, one, 0)

    def gather(size, me, make):
        def one(off, carry):
            src = lax.rem(me + off, size)
            make(src, src, src).wait_recv()
            return carry
        lax.fori_loop(1, size, one, 0)

    lane = pl.ds(pl.multiple_of(r * nj, nj), nj)

    def rows_of(b):
        return pl.ds(pl.multiple_of(b * ni, ni), ni)

    def g1(to, slot, src):
        return remote(gt.at[slot, :, lane], gfull.at[r, rows_of(src)],
                      g1_s.at[slot], g1_r.at[src], "col", to)

    def g2(to, slot, src):
        return remote(gfull.at[src], gfull.at[src], g2_s.at[slot], g2_r.at[src], "row", to)

    def wfc(to, slot, src):
        return remote(wt, wf.at[src], wf_s.at[slot], wf_r.at[src], "ch", to)

    def lrc(to, slot, src):
        return remote(lrs.at[slot], lrr.at[src], lr_s.at[slot], lr_r.at[src], "col", to)

    def dc(to, slot, src):
        return remote(dsend.at[slot], drecv.at[src], d_s.at[slot], d_r.at[src], "col", to)

    def ac(to, slot, src):
        return remote(asend.at[slot], arecv.at[src], a_s.at[slot], a_r.at[src], "ch", to)

    def wa(to, slot, src):
        return remote(ws.at[slot], wr.at[src], wa_s.at[slot], wa_r.at[src], "col", to)

    def wb(to, slot, src):
        return remote(xr.at[src], xr.at[src], wb_s.at[slot], wb_r.at[src], "row", to)

    def wc(to, slot, src):
        return remote(wg.at[src], wg.at[src], wc_s.at[slot], wc_r.at[src], "col", to)

    spread(nc, c, g1)
    spread(nq, q, wfc)
    gfull[r, rows_of(c)] = gt[c, :, lane]
    wf[q] = wt[...]

    tok_k = tok_v[pl.ds(r, 1), :]
    gain_v = gain[...]

    def mask_of(i):
        return (pm[pl.ds(i, 1), :] * tok_k * tok_s[c * ni + i]).astype(F32)

    def project(i, carry):
        std, _ = normalise(pair[i].astype(F32))
        nb = (std * gain_v).astype(BF16)
        normed[i] = nb
        p = lax.dot_general(wt[...], nb, NT, preferred_element_type=F32)
        p = p.reshape(4, hq, nk)
        f, left, right = factors((p[0], p[1], p[2], p[3]), mask_of(i))
        for g in range(4):
            fac[i, g] = f[g]
        lt[i] = left
        rt[i] = right
        return carry

    lax.fori_loop(0, ni, project, 0, unroll=4)

    for h in range(hq):
        lrs[h, 0] = lt[:, h, :].astype(BF16)
        lrs[h, 1] = rt[:, h, :].astype(BF16)
    spread(nc, c, lrc)
    lrr[c] = lrs[c]

    gather(nc, c, g1)
    spread(nr, r, g2)

    gather(nq, q, wfc)

    def own(t, carry):
        i = q * t_n + t
        std, inv = normalise(pair[i].astype(F32))
        stdo[t] = std
        invo[t] = jnp.broadcast_to(inv, (nk, cc))
        p = lax.dot_general(wf[...].reshape(nq * 4 * hq, cc), normed[i], NT,
                            preferred_element_type=F32)
        p = p.reshape(nq, 4, hq, nk)
        f, _, _ = factors((p[:, 0], p[:, 1], p[:, 2], p[:, 3]), mask_of(i))
        for g in range(4):
            fo[t, g] = f[g]
        return carry

    lax.fori_loop(0, t_n, own, 0)

    gather(nr, r, g2)
    gather(nc, c, lrc)

    left_all = lrr[:, 0].reshape(n, nk)
    dl = jnp.zeros((n, nk), F32)
    for x in range(nr):
        rx = lrr[x * jpb:(x + 1) * jpb, 1].reshape(nj, nk)
        dl = dl + jnp.dot(gfull[x], rx, preferred_element_type=F32)
        dr = lax.dot_general(gfull[x], left_all, TN, preferred_element_type=F32)
        dsend[x * jpb:(x + 1) * jpb, 1] = dr.astype(BF16).reshape(jpb, ni, nk)
    dsend[:, 0] = dl.astype(BF16).reshape(nc, ni, nk)
    spread(nc, c, dc)
    drecv[c] = dsend[c]
    gather(nc, c, dc)

    for side in range(2):
        df[side] = drecv[:, side].astype(F32)
    for b in range(nq):
        for t in range(t_n):
            for side in range(2):
                asend[b, side, t] = df[side, :, b * t_n + t, :].astype(BF16)
    spread(nq, q, ac)
    arecv[q] = asend[q]

    def weigh(i, acc):
        b = i // t_n
        t = i - b * t_n
        d0 = asend[b, 0, t].astype(F32)
        d1 = asend[b, 1, t].astype(F32)
        f = fac[i]
        gr = jnp.concatenate([d0 * f[0], d0 * f[1], d1 * f[2], d1 * f[3]], axis=0).astype(BF16)
        return acc + jnp.dot(gr, normed[i], preferred_element_type=F32)

    w_part = lax.fori_loop(0, ni, weigh, jnp.zeros((4 * hq, cc), F32), unroll=4)
    wrows = 4 * hq // nc
    for b in range(nc):
        ws[b] = jnp.concatenate(
            [w_part[b * wrows:(b + 1) * wrows], jnp.zeros((8 - wrows, cc), F32)], axis=0)
    spread(nc, c, wa)
    wr[c] = ws[c]

    gather(nq, q, ac)

    def to_right(b, t):
        return remote(ag.at[b, t], ag.at[b, t], ag_s.at[0, b, t], ag_r.at[b, t], "ch",
                      lax.rem(q + 1, nq))

    def to_left(b, t):
        return remote(ag.at[b, t], ag.at[b, t], ag_s.at[1, b, t], ag_r.at[b, t], "ch",
                      lax.rem(q + nq - 1, nq))

    def back(t, carry):
        d0 = arecv[:, 0, t].astype(F32)
        d1 = arecv[:, 1, t].astype(F32)
        f = fo[t]
        gr = jnp.stack([d0 * f[0], d0 * f[1], d1 * f[2], d1 * f[3]], axis=1).astype(BF16)
        d_norm = lax.dot_general(gr.reshape(nq * 4 * hq, nk), wf[...].reshape(nq * 4 * hq, cc),
                                 TN, preferred_element_type=F32)
        e = d_norm * gain_v
        std = stdo[t]
        first = jnp.mean(e, axis=-1, keepdims=True)
        second = jnp.mean(e * std, axis=-1, keepdims=True)
        ag[q, t] = (invo[t] * (e - first - std * second)).astype(BF16)

        @pl.when(q < nq - 1)
        def _():
            to_right(q, t).start()

        @pl.when(q > 0)
        def _():
            to_left(q, t).start()
        return carry

    lax.fori_loop(0, t_n, back, 0)

    def relay(s):
        def one(t, carry):
            @pl.when(q >= s)
            def _():
                to_right(q - s, t).wait_recv()

                @pl.when(q < nq - 1)
                def _():
                    to_right(q - s, t).start()

            @pl.when(q + s < nq)
            def _():
                to_left(q + s, t).wait_recv()

                @pl.when(q > 0)
                def _():
                    to_left(q + s, t).start()
            return carry
        lax.fori_loop(0, t_n, one, 0)

    gather(nc, c, wa)
    xr[r] = jnp.sum(wr[...], axis=0)
    spread(nr, r, wb)
    relay(1)
    gather(nr, r, wb)
    total = xr[0]
    for x in range(1, nr):
        total = total + xr[x]
    wg[c] = total * (1.0 / n)
    spread(nc, c, wc)
    for s in range(2, nq):
        relay(s)
    gather(nc, c, wc)
    for b in range(nc):
        wout[b * wrows:(b + 1) * wrows, :] = wg[b, :wrows, :]
    out[...] = ag[...].reshape(ni, nk, cc)

    spread(nc, c, g1, False)
    spread(nq, q, wfc, False)
    spread(nc, c, lrc, False)
    spread(nr, r, g2, False)
    spread(nc, c, dc, False)
    spread(nq, q, ac, False)
    spread(nc, c, wa, False)
    spread(nr, r, wb, False)
    spread(nc, c, wc, False)

    def drain(b, carry):
        def one(t, carry):
            @pl.when(jnp.logical_and(b <= q, q < nq - 1))
            def _():
                to_right(b, t).wait_send()

            @pl.when(jnp.logical_and(b >= q, q > 0))
            def _():
                to_left(b, t).wait_send()
            return carry
        return lax.fori_loop(0, t_n, one, carry)
    lax.fori_loop(0, nq, drain, 0)


def body(nr, nc, nq, pair, token_mask, pair_mask, ln_gain, w_in, grad_tri):
    ni, nk, cc = pair.shape
    hq = w_in.shape[2]
    n = nc * ni
    nj = n // nr
    t_n = ni // nq
    wt = jnp.transpose(w_in, (1, 2, 0)).reshape(4 * hq, cc)
    vmem = pl.BlockSpec(memory_space=pltpu.VMEM)
    smem = pl.BlockSpec(memory_space=pltpu.SMEM)
    dma = lambda *s: pltpu.SemaphoreType.DMA(s)
    out, wout = pl.pallas_call(
        functools.partial(kernel, nr, nc, nq),
        out_shape=(
            jax.ShapeDtypeStruct((ni, nk, cc), BF16),
            jax.ShapeDtypeStruct((4 * hq, cc), F32),
        ),
        in_specs=[smem] + [vmem] * 6,
        out_specs=(vmem, vmem),
        scratch_shapes=[
            pltpu.VMEM((ni, nk, cc), BF16),
            pltpu.VMEM((ni, 4, hq, nk), F32),
            pltpu.VMEM((ni, hq, nk), F32),
            pltpu.VMEM((ni, hq, nk), F32),
            pltpu.VMEM((nc, 2, ni, nk), BF16),
            pltpu.VMEM((nc, 2, ni, nk), BF16),
            pltpu.VMEM((nr, n, nj), BF16),
            pltpu.VMEM((nc, 2, ni, nk), BF16),
            pltpu.VMEM((nc, 2, ni, nk), BF16),
            pltpu.VMEM((2, hq, ni, nk), F32),
            pltpu.VMEM((nq, 2, t_n, hq, nk), BF16),
            pltpu.VMEM((nq, 2, t_n, hq, nk), BF16),
            pltpu.VMEM((nq, 4 * hq, cc), BF16),
            pltpu.VMEM((t_n, 4, nq, hq, nk), F32),
            pltpu.VMEM((t_n, nk, cc), F32),
            pltpu.VMEM((t_n, nk, cc), F32),
            pltpu.VMEM((nq, t_n, nk, cc), BF16),
            pltpu.VMEM((nc, 8, cc), F32),
            pltpu.VMEM((nc, 8, cc), F32),
            pltpu.VMEM((nr, 8, cc), F32),
            pltpu.VMEM((nc, 8, cc), F32),
            dma(nc), dma(nc), dma(nr), dma(nr), dma(nq), dma(nq),
            dma(nc), dma(nc), dma(nc), dma(nc), dma(nq), dma(nq),
            dma(2, nq, t_n), dma(nq, t_n),
            dma(nc), dma(nc), dma(nr), dma(nr), dma(nc), dma(nc),
        ],
        compiler_params=pltpu.CompilerParams(
            collective_id=0, has_side_effects=True, vmem_limit_bytes=48 * 1024 * 1024,
        ),
        name="triangle_backward",
    )(token_mask, token_mask.reshape(nr, nk), pair, pair_mask, ln_gain.reshape(1, cc), wt, grad_tri)
    w_grad = jnp.transpose(wout.reshape(4, hq, cc), (2, 0, 1))
    return out, w_grad


def solution(mesh):
    size = dict(mesh.shape)
    return jax.shard_map(
        functools.partial(body, size["row"], size["col"], size["ch"]),
        mesh=mesh,
        in_specs=(
            P("col", "row", None),
            P(),
            P("col", "row"),
            P(),
            P(None, None, "ch"),
            P("ch", "col", None),
        ),
        out_specs=(P("col", "row", None), P(None, None, "ch")),
        check_vma=False,
    )
```

time: 843 us -> 116 us (0.14); the launches traced: 827 us -> 115 us
  blocking collectives: 542 us -> 0 us
  waiting for transfers between devices: 241 us -> 0 us
  Pallas kernels: 0 us -> 108 us
  other arithmetic: 15.5 us -> 0 us
  between operations: 13.9 us -> 0.66 us
  matrix products: 9.49 us -> 0 us
    psum x1 -> x0, blocking collectives: 542 us -> none  [body(): w_grad = lax.psum(weight_part, ('row', 'col')) / full_n]
    reduce_scatter x1 -> x0, waiting for transfers between devices: 143 us -> none  [body(): lax.psum_scatter(jnp.einsum('hij,hik->jhk', grad_part, left, preferred_el...]
    pallas_call x0 -> x1, Pallas kernels: none -> 108 us  [body(): pl.pallas_call(functools.partial(kernel, nr, nc, nq), out_shape=(jax.Shap...]
    all_gather x1 -> x0, waiting for transfers between devices: 98 us -> none  [body(): lax.all_gather(right, 'col', axis=1, tiled=True)]
    dot_general x5 -> x0, matrix products: 9.49 us -> none  [the longest x1 2.72 us: body(): jnp.einsum('hij,hik->jhk', grad_part, left, preferred_element_type=jnp.fl...]
  transfers between devices with their start and end apart: 3 -> 0, of which waited for: 2 -> 0; matrix products, arithmetic and copies ran while one was open for 0% -> 0% of each run, Pallas kernels for 0% -> 0%
where the time goes in v1:
time: 116 us; the launch traced here: 115 us
  Pallas kernels  108 us (93%)
  local copies, waits for them, and re-layouts  5.96 us (5%)
    pallas_call x1, Pallas kernels, body(): pl.pallas_call(functools.partial(kernel, nr, nc, nq), out_shape=(jax.Shap...  108 us
    unnamed x14, local copies, waits for them, and re-layouts  5.96 us

profile of v1, /device:TPU:1, one launch (start us, length us, event | category | flops | bytes accessed | tf_op | source)
XLA Modules:
  0.0 114.6 jit_solution(13026550356603509655)
XLA Ops:
  0.6 0.0 copy-start.4
  0.6 0.0 copy-start.5
  0.7 0.7 copy-done.4
  1.3 0.0 copy-done.5
  1.3 0.0 copy-start
  1.3 1.2 %copy-done = bf16[32,128,128]{2,1,0:T(8,128)(2,1)S(1)} copy-done((bf16[32,128,128]{2,1,0:T(8,128)(2,1)S(1)}, bf16[32,128,128]{2,1,0:T(8,128)(2,1)}, u32[]{:S(2)}) %copy-start) | copy-done | bytes 1048600
  2.5 0.0 copy-start.1
  2.5 1.0 copy-done.1
  3.6 0.0 copy-start.2
  3.6 0.7 copy-done.2
  4.3 0.0 copy-start.3
  4.3 0.7 copy-done.3
  5.0 108.0 %triangle_backward.1 = (bf16[32,128,128]{2,1,0:T(8,128)(2,1)S(1)}, f32[64,128]{1,0:T(8,128)S(1)}) custom-call(s32[512]{0:T(512)S(1)} %copy-done.4, s32[4,128]{1,0:T(4,128)S(1)} %bitcast.10, bf16[32,128,128]{2,1,0:T(8,128)(2,1)S(1)} %copy-done, s32[32,128]{1,0:T(8,128)S(1)} %copy-done.2, f32[1,128]{1,0:T(1,128)S(1)} %bitcast.11, bf16[64,128]{1,0:T(8,128)(2,1)S(1)} %bitcast.9, ...), custom_call_target="tpu_custom_call" | custom-call | tf_op jit(solution)/shard_map/triangle_backward/pallas_call | solution.py:324
  113.1 1.0 copy.10
  114.0 0.6 copy.11
Async XLA Ops:
  0.6 0.7 copy-start.4
  0.6 0.7 copy-start.5
  1.3 1.2 %copy-start = (bf16[32,128,128]{2,1,0:T(8,128)(2,1)S(1)}, bf16[32,128,128]{2,1,0:T(8,128)(2,1)}, u32[]{:S(2)}) copy-start(bf16[32,128,128]{2,1,0:T(8,128)(2,1)} %pair.1) | copy-start | bytes 3145732
  2.5 1.0 copy-start.1
  3.6 0.7 copy-start.2
  4.3 0.7 copy-start.3

commit v2 on v1

v2 whole, which is shorter than its diff:
```python
import functools

import jax
import jax.numpy as jnp
from jax import lax
from jax.experimental import pallas as pl
from jax.experimental.pallas import tpu as pltpu
from jax.sharding import PartitionSpec as P

EPS = 1e-05
F32 = jnp.float32
BF16 = jnp.bfloat16
MESH = pl.DeviceIdType.MESH
NT = (((1,), (1,)), ((), ()))
TN = (((0,), (0,)), ((), ()))


def normalise(x):
    mean = jnp.mean(x, axis=-1, keepdims=True)
    cen = x - mean
    inv = lax.rsqrt(jnp.mean(cen * cen, axis=-1, keepdims=True) + EPS)
    return cen * inv, inv


def factors(p, m):
    p0, p1, p2, p3 = p
    s1 = jax.nn.sigmoid(p1)
    s3 = jax.nn.sigmoid(p3)
    f0 = m * s1
    f2 = m * s3
    return f0, f0 * p0 * (1.0 - s1), f2, f2 * p2 * (1.0 - s3)


def kernel(
    nr, nc, nq,
    tok, pair_h, pm_h, gain_h, w_h, gt,
    out, wout,
    tok_v, pair, pm, gain, w_v, mask, wt,
    normed, lt, rt, lrs, lrr, gfull, dsend, drecv, df, asend, arecv,
    wf, fo, stdo, invo, gro, ag, wp, wr, zp, zr, xr, wg,
    in_s, o_s,
    g1_s, g1_r, g2_s, g2_r, wf_s, wf_r, lr_s, lr_r, d_s, d_r, a_s, a_r,
    ag_s, ag_r, wa_s, wa_r, wb_s, wb_r, wc_s, wc_r, wd_s, wd_r,
):
    r = lax.axis_index("row")
    c = lax.axis_index("col")
    q = lax.axis_index("ch")
    ni, nk, cc = pair.shape
    hq = nc
    n = nc * ni
    nj = gfull.shape[2]
    t_n = ni // nq
    jpb = nj // ni
    npl = nc // 2
    nz = 2 * nq
    zh = lax.rem(lax.div(c, 2), 2)
    m = lax.div(c, 4) * 2 + lax.rem(c, 2)
    z = zh * nq + q

    def col_of(zh_, m_):
        return (lax.div(m_, 2) * 2 + zh_) * 2 + lax.rem(m_, 2)

    def pos(c_):
        return lax.rem(lax.div(c_, 2), 2) * npl + lax.div(c_, 4) * 2 + lax.rem(c_, 2)

    def to_row(i):
        return {"row": i}

    def to_col(i):
        return {"col": i}

    def to_ch(i):
        return {"ch": i}

    def to_plane(i):
        return {"col": col_of(zh, i)}

    def to_z(i):
        return {"col": col_of(lax.div(i, nq), m), "ch": lax.rem(i, nq)}

    loads = [
        pltpu.make_async_copy(src, dst, in_s.at[k])
        for k, (src, dst) in enumerate(
            ((w_h, w_v), (tok, tok_v), (pm_h, pm), (gain_h, gain), (pair_h, pair)))
    ]
    for load in loads:
        load.start()

    barrier = pltpu.get_barrier_semaphore()

    def greet(device):
        pl.semaphore_signal(barrier, inc=1, device_id=device, device_id_type=MESH)

    def greet_all(size, me, to):
        def one(off, carry):
            greet(to(lax.rem(me + off, size)))
            return carry
        lax.fori_loop(1, size, one, 0)

    greet_all(nr, r, to_row)
    greet_all(nc, c, to_col)
    greet_all(nq, q, to_ch)

    def greet_far(off, carry):
        greet({"col": col_of(1 - zh, m), "ch": lax.rem(q + off, nq)})
        return carry
    lax.fori_loop(1, nq, greet_far, 0)

    for load in loads:
        load.wait()

    def permuted(w):
        rows = []
        for g in range(4):
            for half in range(2):
                for y in range(nc // 4):
                    at = g * hq + (y * 2 + half) * 2
                    rows.append(w[at:at + 2])
        return jnp.concatenate(rows, axis=0)

    def natural(w):
        rows = []
        for g in range(4):
            for y in range(nc // 4):
                for half in range(2):
                    at = g * hq + half * npl + y * 2
                    rows.append(w[at:at + 2])
        return jnp.concatenate(rows, axis=0)

    wv = permuted(w_v[...].astype(F32)).astype(BF16)
    wt[...] = wv
    wf[q] = wv

    tok_k = tok_v[pl.ds(r, 1), :]
    first = c * ni
    tok_i = tok_v[pl.ds(lax.div(first, nk), 1), :]
    at = lax.broadcasted_iota(jnp.int32, (ni, nk), 1) - lax.rem(first, nk)
    hit = at == lax.broadcasted_iota(jnp.int32, (ni, nk), 0)
    tok_i = jnp.sum(jnp.where(hit, tok_i, 0).astype(F32), axis=1, keepdims=True)
    mask[...] = (pm[...] * tok_k).astype(F32) * tok_i
    gain_v = gain[...]

    pl.semaphore_wait(barrier, nr + nc + 2 * nq - 4)

    def remote(src, dst, s, rr, device):
        return pltpu.make_async_remote_copy(
            src_ref=src, dst_ref=dst, send_sem=s, recv_sem=rr,
            device_id=device, device_id_type=MESH,
        )

    def spread(size, me, make, start=True):
        def one(off, carry):
            to = lax.rem(me + off, size)
            copy = make(to, me)
            if start:
                copy.start()
            else:
                copy.wait_send()
            return carry
        lax.fori_loop(1, size, one, 0)

    def gather(size, me, make):
        def one(off, carry):
            src = lax.rem(me + off, size)
            make(src, src).wait_recv()
            return carry
        lax.fori_loop(1, size, one, 0)

    lane = pl.ds(pl.multiple_of(r * nj, nj), nj)

    def rows_of(b):
        return pl.ds(pl.multiple_of(b * ni, ni), ni)

    def g1(to, src):
        return remote(gt.at[to, :, lane], gfull.at[r, rows_of(src)],
                      g1_s.at[to], g1_r.at[src], to_col(to))

    def g2(to, src):
        return remote(gfull.at[src], gfull.at[src], g2_s.at[to], g2_r.at[src], to_row(to))

    def wfc(to, src):
        return remote(wt, wf.at[src], wf_s.at[to], wf_r.at[src], to_ch(to))

    def lrc(to, src):
        return remote(lrs.at[pos(to)], lrr.at[src], lr_s.at[to], lr_r.at[src], to_col(to))

    def dc(to, src):
        return remote(dsend.at[to], drecv.at[src], d_s.at[to], d_r.at[src], to_plane(to))

    def ac(to, src):
        return remote(asend.at[to], arecv.at[src], a_s.at[to], a_r.at[src], to_z(to))

    def wa(to, src):
        return remote(wp.at[to], wr.at[src], wa_s.at[to], wa_r.at[src], to_plane(to))

    def wb(to, src):
        return remote(zp.at[lax.rem(to, nq)], zr.at[src], wb_s.at[to], wb_r.at[src], to_z(to))

    def wc(to, src):
        return remote(xr.at[src], xr.at[src], wc_s.at[to], wc_r.at[src], to_row(to))

    def wd(to, src):
        return remote(wg.at[src], wg.at[src], wd_s.at[to], wd_r.at[src], to_plane(to))

    spread(nc, c, g1)
    spread(nq, q, wfc)
    mine = pltpu.make_async_copy(gt.at[c, :, lane], gfull.at[r, rows_of(c)], g1_s.at[c])
    mine.start()

    def mask_of(i):
        return mask[pl.ds(i, 1), :]

    def project(i, carry):
        std, _ = normalise(pair[i].astype(F32))
        nb = (std * gain_v).astype(BF16)
        normed[i] = nb
        p = lax.dot_general(wt[...], nb, NT, preferred_element_type=F32)
        p = p.reshape(4, hq, nk)
        mk = mask_of(i)
        lt[i] = mk * jax.nn.sigmoid(p[1]) * p[0]
        rt[i] = mk * jax.nn.sigmoid(p[3]) * p[2]
        return carry

    lax.fori_loop(0, ni, project, 0, unroll=4)

    for h in range(hq):
        lrs[h, 0] = lt[:, h, :].astype(BF16)
        lrs[h, 1] = rt[:, h, :].astype(BF16)
    spread(nc, c, lrc)
    lrr[c] = lrs[pos(c)]

    gather(nq, q, wfc)

    def own(t, carry):
        i = q * t_n + t
        std, inv = normalise(pair[i].astype(F32))
        stdo[t] = std
        invo[t] = jnp.broadcast_to(inv, (nk, cc))
        p = lax.dot_general(wf[...].reshape(nq * 4 * hq, cc), normed[i], NT,
                            preferred_element_type=F32)
        p = p.reshape(nq, 4, hq, nk)
        f = factors((p[:, 0], p[:, 1], p[:, 2], p[:, 3]), mask_of(i))
        for g in range(4):
            fo[t, g] = f[g]
        return carry

    lax.fori_loop(0, t_n, own, 0)

    gather(nc, c, g1)
    mine.wait()
    spread(nr, r, g2)
    gather(nr, r, g2)
    gather(nc, c, lrc)

    left_all = lrr[:, 0].reshape(n, nk)
    dl = jnp.zeros((n, nk), F32)
    for x in range(nr):
        rx = lrr[x * jpb:(x + 1) * jpb, 1].reshape(nj, nk)
        dl = dl + jnp.dot(gfull[x], rx, preferred_element_type=F32)
        dr = lax.dot_general(gfull[x], left_all, TN, preferred_element_type=F32)
        dr = dr.astype(BF16).reshape(jpb, ni, nk)
        for b in range(jpb):
            cb = x * jpb + b
            dsend[cb // 4 * 2 + cb % 2, cb // 2 % 2, 1] = dr[b]
    dl = dl.astype(BF16).reshape(nc, ni, nk)
    for cb in range(nc):
        dsend[cb // 4 * 2 + cb % 2, cb // 2 % 2, 0] = dl[cb]
    spread(npl, m, dc)
    drecv[m] = dsend[m]
    gather(npl, m, dc)

    for half in range(2):
        for side in range(2):
            df[half, side] = drecv[:, half, side].astype(F32)
    for half in range(2):
        for b in range(nq):
            for t in range(t_n):
                i = b * t_n + t
                asend[half * nq + b, t] = jnp.concatenate(
                    [df[half, 0, :, i, :], df[half, 1, :, i, :]], axis=0).astype(BF16)
    spread(nz, z, ac)
    arecv[z] = asend[z]
    gather(nz, z, ac)

    def to_right(b, t):
        return remote(ag.at[b, t], ag.at[b, t], ag_s.at[0, b, t], ag_r.at[b, t],
                      to_ch(lax.rem(q + 1, nq)))

    def to_left(b, t):
        return remote(ag.at[b, t], ag.at[b, t], ag_s.at[1, b, t], ag_r.at[b, t],
                      to_ch(lax.rem(q + nq - 1, nq)))

    def keep(b, t):
        return pltpu.make_async_copy(ag.at[b, t], out.at[b * t_n + t], o_s.at[b, t])

    for t in range(t_n):
        d = jnp.stack([
            jnp.stack([arecv[half * nq + b, t].astype(F32) for half in range(2)])
            for b in range(nq)])
        d0 = d[:, :, :npl].reshape(nq, hq, nk)
        d1 = d[:, :, npl:].reshape(nq, hq, nk)
        f = fo[t]
        gr = jnp.stack([d0 * f[0], d0 * f[1], d1 * f[2], d1 * f[3]], axis=1)
        gr = gr.reshape(nq * 4 * hq, nk).astype(BF16)
        gro[:, t * nk:(t + 1) * nk] = gr
        d_norm = lax.dot_general(gr, wf[...].reshape(nq * 4 * hq, cc),
                                 TN, preferred_element_type=F32)
        e = d_norm * gain_v
        std = stdo[t]
        first = jnp.mean(e, axis=-1, keepdims=True)
        second = jnp.mean(e * std, axis=-1, keepdims=True)
        ag[q, t] = (invo[t] * (e - first - std * second)).astype(BF16)
        keep(q, t).start()

        @pl.when(q < nq - 1)
        def _():
            to_right(q, t).start()

        @pl.when(q > 0)
        def _():
            to_left(q, t).start()

    nb = normed[pl.ds(q * t_n, t_n)].reshape(t_n * nk, cc)
    w_part = jnp.dot(gro[...], nb, preferred_element_type=F32).reshape(nq, npl, 8, cc)
    for b in range(npl):
        wp[b] = w_part[:, b]
    spread(npl, m, wa)
    wr[m] = wp[m]

    def relay(s):
        def one(t, carry):
            @pl.when(q >= s)
            def _():
                to_right(q - s, t).wait_recv()

                @pl.when(q < nq - 1)
                def _():
                    to_right(q - s, t).start()
                keep(q - s, t).start()

            @pl.when(q + s < nq)
            def _():
                to_left(q + s, t).wait_recv()

                @pl.when(q > 0)
                def _():
                    to_left(q + s, t).start()
                keep(q + s, t).start()
            return carry
        lax.fori_loop(0, t_n, one, 0)

    relay(1)
    gather(npl, m, wa)
    zp[...] = jnp.sum(wr[...], axis=0)
    spread(nz, z, wb)
    zr[z] = zp[q]
    for s in range(2, max(3, nq - 3)):
        if s < nq:
            relay(s)
    gather(nz, z, wb)
    xr[r] = jnp.sum(zr[...], axis=0)
    spread(nr, r, wc)
    for s in range(max(3, nq - 3), nq - 1):
        relay(s)
    gather(nr, r, wc)
    total = xr[0]
    for x in range(1, nr):
        total = total + xr[x]
    wg[m] = total * (1.0 / n)
    spread(npl, m, wd)
    if nq - 1 >= max(3, nq - 3):
        relay(nq - 1)
    gather(npl, m, wd)
    wout[...] = natural(wg[...].reshape(4 * hq, cc))

    spread(nc, c, g1, False)
    spread(nq, q, wfc, False)
    spread(nc, c, lrc, False)
    spread(nr, r, g2, False)
    spread(npl, m, dc, False)
    spread(nz, z, ac, False)
    spread(npl, m, wa, False)
    spread(nz, z, wb, False)
    spread(nr, r, wc, False)
    spread(npl, m, wd, False)

    def drain(b, carry):
        def one(t, carry):
            @pl.when(jnp.logical_and(b <= q, q < nq - 1))
            def _():
                to_right(b, t).wait_send()

            @pl.when(jnp.logical_and(b >= q, q > 0))
            def _():
                to_left(b, t).wait_send()
            keep(b, t).wait()
            return carry
        return lax.fori_loop(0, t_n, one, carry)
    lax.fori_loop(0, nq, drain, 0)


def body(nr, nc, nq, pair, token_mask, pair_mask, ln_gain, w_in, grad_tri):
    ni, nk, cc = pair.shape
    hq = w_in.shape[2]
    n = nc * ni
    nj = n // nr
    t_n = ni // nq
    npl = nc // 2
    nz = 2 * nq
    wt = jnp.transpose(w_in, (1, 2, 0)).reshape(4 * hq, cc)
    vmem = pl.BlockSpec(memory_space=pltpu.VMEM)
    hbm = pl.BlockSpec(memory_space=pltpu.HBM)
    dma = lambda *s: pltpu.SemaphoreType.DMA(s)
    out, wout = pl.pallas_call(
        functools.partial(kernel, nr, nc, nq),
        out_shape=(
            jax.ShapeDtypeStruct((ni, nk, cc), BF16),
            jax.ShapeDtypeStruct((4 * hq, cc), F32),
        ),
        in_specs=[hbm] * 6,
        out_specs=(hbm, vmem),
        scratch_shapes=[
            pltpu.VMEM((n // nk, nk), jnp.int32),
            pltpu.VMEM((ni, nk, cc), BF16),
            pltpu.VMEM((ni, nk), jnp.int32),
            pltpu.VMEM((1, cc), F32),
            pltpu.VMEM((4 * hq, cc), BF16),
            pltpu.VMEM((ni, nk), F32),
            pltpu.VMEM((4 * hq, cc), BF16),
            pltpu.VMEM((ni, nk, cc), BF16),
            pltpu.VMEM((ni, hq, nk), F32),
            pltpu.VMEM((ni, hq, nk), F32),
            pltpu.VMEM((nc, 2, ni, nk), BF16),
            pltpu.VMEM((nc, 2, ni, nk), BF16),
            pltpu.VMEM((nr, n, nj), BF16),
            pltpu.VMEM((npl, 2, 2, ni, nk), BF16),
            pltpu.VMEM((npl, 2, 2, ni, nk), BF16),
            pltpu.VMEM((2, 2, npl, ni, nk), F32),
            pltpu.VMEM((nz, t_n, hq, nk), BF16),
            pltpu.VMEM((nz, t_n, hq, nk), BF16),
            pltpu.VMEM((nq, 4 * hq, cc), BF16),
            pltpu.VMEM((t_n, 4, nq, hq, nk), F32),
            pltpu.VMEM((t_n, nk, cc), F32),
            pltpu.VMEM((t_n, nk, cc), F32),
            pltpu.VMEM((nq * 4 * hq, t_n * nk), BF16),
            pltpu.VMEM((nq, t_n, nk, cc), BF16),
            pltpu.VMEM((npl, nq, 8, cc), F32),
            pltpu.VMEM((npl, nq, 8, cc), F32),
            pltpu.VMEM((nq, 8, cc), F32),
            pltpu.VMEM((nz, 8, cc), F32),
            pltpu.VMEM((nr, 8, cc), F32),
            pltpu.VMEM((npl, 8, cc), F32),
            dma(5), dma(nq, t_n),
            dma(nc), dma(nc), dma(nr), dma(nr), dma(nq), dma(nq),
            dma(nc), dma(nc), dma(npl), dma(npl), dma(nz), dma(nz),
            dma(2, nq, t_n), dma(nq, t_n),
            dma(npl), dma(npl), dma(nz), dma(nz), dma(nr), dma(nr), dma(npl), dma(npl),
        ],
        compiler_params=pltpu.CompilerParams(
            collective_id=0, has_side_effects=True, vmem_limit_bytes=48 * 1024 * 1024,
        ),
        name="triangle_backward",
    )(token_mask.reshape(n // nk, nk), pair, pair_mask, ln_gain.reshape(1, cc), wt, grad_tri)
    w_grad = jnp.transpose(wout.reshape(4, hq, cc), (2, 0, 1))
    return out, w_grad


def solution(mesh):
    size = dict(mesh.shape)
    return jax.shard_map(
        functools.partial(body, size["row"], size["col"], size["ch"]),
        mesh=mesh,
        in_specs=(
            P("col", "row", None),
            P(),
            P("col", "row"),
            P(),
            P(None, None, "ch"),
            P("ch", "col", None),
        ),
        out_specs=(P("col", "row", None), P(None, None, "ch")),
        check_vma=False,
    )
```

time: 116 us -> 108 us (0.931); the launches traced: 115 us -> 108 us
  Pallas kernels: 108 us -> 101 us
    pallas_call x1, Pallas kernels: 108 us -> 101 us  [body(): pl.pallas_call(functools.partial(kernel, nr, nc, nq), out_shape=(jax.Shap...]
where the time goes in v2:
time: 108 us
  Pallas kernels  101 us (94%)
  local copies, waits for them, and re-layouts  5.96 us (6%)
    pallas_call x1, Pallas kernels, body(): pl.pallas_call(functools.partial(kernel, nr, nc, nq), out_shape=(jax.Shap...  101 us
    unnamed x14, local copies, waits for them, and re-layouts  5.96 us

profile of v2, /device:TPU:1, one launch (start us, length us, event | category | flops | bytes accessed | tf_op | source)
XLA Modules:
  0.0 108.0 jit_solution(14602071325543382082)
XLA Ops:
  0.6 0.0 copy-start.4
  0.6 0.0 copy-start.5
  0.7 0.7 copy-done.4
  1.3 0.0 copy-done.5
  1.3 0.0 copy-start
  1.3 1.2 %copy-done = bf16[32,128,128]{2,1,0:T(8,128)(2,1)S(1)} copy-done((bf16[32,128,128]{2,1,0:T(8,128)(2,1)S(1)}, bf16[32,128,128]{2,1,0:T(8,128)(2,1)}, u32[]{:S(2)}) %copy-start) | copy-done | bytes 1048600
  2.5 0.0 copy-start.1
  2.5 1.0 copy-done.1
  3.6 0.0 copy-start.2
  3.6 0.7 copy-done.2
  4.3 0.0 copy-start.3
  4.3 0.7 copy-done.3
  5.0 101.4 %triangle_backward.1 = (bf16[32,128,128]{2,1,0:T(8,128)(2,1)S(1)}, f32[64,128]{1,0:T(8,128)S(1)}) custom-call(s32[4,128]{1,0:T(4,128)S(1)} %bitcast.10, bf16[32,128,128]{2,1,0:T(8,128)(2,1)S(1)} %copy-done, s32[32,128]{1,0:T(8,128)S(1)} %copy-done.2, f32[1,128]{1,0:T(1,128)S(1)} %bitcast.11, bf16[64,128]{1,0:T(8,128)(2,1)S(1)} %bitcast.9, ...), custom_call_target="tpu_custom_call" | custom-call | tf_op jit(solution)/shard_map/triangle_backward/pallas_call | solution.py:414
  106.4 1.0 copy.10
  107.4 0.6 copy.11
Async XLA Ops:
  0.6 0.7 copy-start.4
  0.6 0.7 copy-start.5
  1.3 1.2 %copy-start = (bf16[32,128,128]{2,1,0:T(8,128)(2,1)S(1)}, bf16[32,128,128]{2,1,0:T(8,128)(2,1)}, u32[]{:S(2)}) copy-start(bf16[32,128,128]{2,1,0:T(8,128)(2,1)} %pair_h.1) | copy-start | bytes 3145732
  2.5 1.0 copy-start.1
  3.6 0.7 copy-start.2
  4.3 0.7 copy-start.3

commit v3 on v2

--- a/solution.py
+++ b/solution.py
@@ -37,10 +37,10 @@
     out, wout,
     tok_v, pair, pm, gain, w_v, mask, wt,
     normed, lt, rt, lrs, lrr, gfull, dsend, drecv, df, asend, arecv,
-    wf, fo, stdo, invo, gro, ag, wp, wr, zp, zr, xr, wg,
+    wf, fo, stdo, invo, gro, ag, wp, wr, zp, zq, zr, xr, wg,
     in_s, o_s,
     g1_s, g1_r, g2_s, g2_r, wf_s, wf_r, lr_s, lr_r, d_s, d_r, a_s, a_r,
-    ag_s, ag_r, wa_s, wa_r, wb_s, wb_r, wc_s, wc_r, wd_s, wd_r,
+    ag_s, ag_r, wa_s, wa_r, wx_s, wx_r, wz_s, wz_r, wb_s, wb_r, wd_s, wd_r,
 ):
     r = lax.axis_index("row")
     c = lax.axis_index("col")
@@ -193,11 +193,22 @@
     def wa(to, src):
         return remote(wp.at[to], wr.at[src], wa_s.at[to], wa_r.at[src], to_plane(to))
 
+    qr = nq // nr
+    owner = lax.div(q, qr) == r
+
+    def wx(to, src):
+        return remote(zp.at[pl.ds(to * qr, qr)], xr.at[src], wx_s.at[to], wx_r.at[src],
+                      to_row(to))
+
+    def wz(half, a):
+        to = half * nq + r * qr + a
+        return to, remote(zq.at[a], zr.at[z], wz_s.at[half, a], wz_r.at[z], to_z(to))
+
+    def wz_from(to, src):
+        return remote(zq.at[0], zr.at[src], wz_s.at[0, 0], wz_r.at[src], to_z(to))
+
     def wb(to, src):
-        return remote(zp.at[lax.rem(to, nq)], zr.at[src], wb_s.at[to], wb_r.at[src], to_z(to))
-
-    def wc(to, src):
-        return remote(xr.at[src], xr.at[src], wc_s.at[to], wc_r.at[src], to_row(to))
+        return remote(wg.at[m], wg.at[m], wb_s.at[to], wb_r.at[0], to_row(to))
 
     def wd(to, src):
         return remote(wg.at[src], wg.at[src], wd_s.at[to], wd_r.at[src], to_plane(to))
@@ -228,6 +239,10 @@
         lrs[h, 1] = rt[:, h, :].astype(BF16)
     spread(nc, c, lrc)
     lrr[c] = lrs[pos(c)]
+
+    gather(nc, c, g1)
+    mine.wait()
+    spread(nr, r, g2)
 
     gather(nq, q, wfc)
 
@@ -246,9 +261,6 @@
 
     lax.fori_loop(0, t_n, own, 0)
 
-    gather(nc, c, g1)
-    mine.wait()
-    spread(nr, r, g2)
     gather(nr, r, g2)
     gather(nc, c, lrc)
 
@@ -320,13 +332,6 @@
         def _():
             to_left(q, t).start()
 
-    nb = normed[pl.ds(q * t_n, t_n)].reshape(t_n * nk, cc)
-    w_part = jnp.dot(gro[...], nb, preferred_element_type=F32).reshape(nq, npl, 8, cc)
-    for b in range(npl):
-        wp[b] = w_part[:, b]
-    spread(npl, m, wa)
-    wr[m] = wp[m]
-
     def relay(s):
         def one(t, carry):
             @pl.when(q >= s)
@@ -349,28 +354,66 @@
             return carry
         lax.fori_loop(0, t_n, one, 0)
 
-    relay(1)
-    gather(npl, m, wa)
-    zp[...] = jnp.sum(wr[...], axis=0)
-    spread(nz, z, wb)
-    zr[z] = zp[q]
-    for s in range(2, max(3, nq - 3)):
-        if s < nq:
-            relay(s)
-    gather(nz, z, wb)
-    xr[r] = jnp.sum(zr[...], axis=0)
-    spread(nr, r, wc)
-    for s in range(max(3, nq - 3), nq - 1):
+    def w_own():
+        nb = normed[pl.ds(q * t_n, t_n)].reshape(t_n * nk, cc)
+        w_part = jnp.dot(gro[...], nb, preferred_element_type=F32).reshape(nq, npl, 8, cc)
+        for b in range(npl):
+            wp[b] = w_part[:, b]
+        spread(npl, m, wa)
+        wr[m] = wp[m]
+
+    def w_plane():
+        gather(npl, m, wa)
+        zp[...] = jnp.sum(wr[...], axis=0)
+        spread(nr, r, wx)
+        xr[r] = zp[pl.ds(r * qr, qr)]
+
+    def w_rows():
+        gather(nr, r, wx)
+        total = xr[0]
+        for x in range(1, nr):
+            total = total + xr[x]
+        zq[...] = total
+        for half in range(2):
+            for a in range(qr):
+                to, copy = wz(half, a)
+
+                @pl.when(to != z)
+                def _(copy=copy):
+                    copy.start()
+
+                @pl.when(to == z)
+                def _(a=a):
+                    zr[z] = zq[a]
+
+    def w_ring():
+        @pl.when(owner)
+        def _():
+            gather(nz, z, wz_from)
+            wg[m] = jnp.sum(zr[...], axis=0) * (1.0 / n)
+            spread(nr, r, wb)
+
+    def w_share():
+        @pl.when(jnp.logical_not(owner))
+        def _():
+            wb(r, r).wait_recv()
+        spread(npl, m, wd)
+
+    def w_last():
+        gather(npl, m, wd)
+
+    steps = {1: [w_own], 2: [w_plane], 3: [w_rows], 5: [w_ring], 6: [w_share]}
+    done = set()
+    for s in range(1, nq):
         relay(s)
-    gather(nr, r, wc)
-    total = xr[0]
-    for x in range(1, nr):
-        total = total + xr[x]
-    wg[m] = total * (1.0 / n)
-    spread(npl, m, wd)
-    if nq - 1 >= max(3, nq - 3):
-        relay(nq - 1)
-    gather(npl, m, wd)
+        for step in steps.get(s, ()):
+            step()
+            done.add(step)
+    for at in sorted(steps):
+        for step in steps[at]:
+            if step not in done:
+                step()
+    w_last()
     wout[...] = natural(wg[...].reshape(4 * hq, cc))
 
     spread(nc, c, g1, False)
@@ -380,8 +423,18 @@
     spread(npl, m, dc, False)
     spread(nz, z, ac, False)
     spread(npl, m, wa, False)
-    spread(nz, z, wb, False)
-    spread(nr, r, wc, False)
+    spread(nr, r, wx, False)
+    for half in range(2):
+        for a in range(qr):
+            to, copy = wz(half, a)
+
+            @pl.when(to != z)
+            def _(copy=copy):
+                copy.wait_send()
+
+    @pl.when(owner)
+    def _():
+        spread(nr, r, wb, False)
     spread(npl, m, wd, False)
 
     def drain(b, carry):
@@ -447,17 +500,19 @@
             pltpu.VMEM((npl, nq, 8, cc), F32),
             pltpu.VMEM((npl, nq, 8, cc), F32),
             pltpu.VMEM((nq, 8, cc), F32),
+            pltpu.VMEM((nq // nr, 8, cc), F32),
             pltpu.VMEM((nz, 8, cc), F32),
-            pltpu.VMEM((nr, 8, cc), F32),
+            pltpu.VMEM((nr, nq // nr, 8, cc), F32),
             pltpu.VMEM((npl, 8, cc), F32),
             dma(5), dma(nq, t_n),
             dma(nc), dma(nc), dma(nr), dma(nr), dma(nq), dma(nq),
             dma(nc), dma(nc), dma(npl), dma(npl), dma(nz), dma(nz),
             dma(2, nq, t_n), dma(nq, t_n),
-            dma(npl), dma(npl), dma(nz), dma(nz), dma(nr), dma(nr), dma(npl), dma(npl),
+            dma(npl), dma(npl), dma(nr), dma(nr), dma(2, nq // nr), dma(nz), dma(nr), dma(1),
+            dma(npl), dma(npl),
         ],
         compiler_params=pltpu.CompilerParams(
-            collective_id=0, has_side_effects=True, vmem_limit_bytes=48 * 1024 * 1024,
+            collective_id=0, has_side_effects=True, vmem_limit_bytes=60 * 1024 * 1024,
         ),
         name="triangle_backward",
     )(token_mask.reshape(n // nk, nk), pair, pair_mask, ln_gain.reshape(1, cc), wt, grad_tri)

time: 108 us -> 103 us (0.954)
  local copies, waits for them, and re-layouts: 5.96 us -> 2.93 us
  Pallas kernels: 101 us -> 99 us
    unnamed x14 -> x4, local copies, waits for them, and re-layouts: 5.96 us -> 2.93 us
    pallas_call x1, Pallas kernels: 101 us -> 99 us  [body(): pl.pallas_call(functools.partial(kernel, nr, nc, nq), out_shape=(jax.Shap...]
where the time goes in v3:
time: 103 us
  Pallas kernels  99 us (96%)
  local copies, waits for them, and re-layouts  2.93 us (3%)
    pallas_call x1, Pallas kernels, body(): pl.pallas_call(functools.partial(kernel, nr, nc, nq), out_shape=(jax.Shap...  99 us
    unnamed x4, local copies, waits for them, and re-layouts  2.93 us

profile of v3, /device:TPU:1, one launch (start us, length us, event | category | flops | bytes accessed | tf_op | source)
XLA Modules:
  0.0 102.6 jit_solution(10999458024541116725)
XLA Ops:
  0.6 99.0 %triangle_backward.1 = (bf16[32,128,128]{2,1,0:T(8,128)(2,1)}, f32[64,128]{1,0:T(8,128)}) custom-call(s32[4,128]{1,0:T(4,128)} %bitcast.10, bf16[32,128,128]{2,1,0:T(8,128)(2,1)} %pair_h.1, s32[32,128]{1,0:T(8,128)} %pm_h.1, f32[1,128]{1,0:T(1,128)} %bitcast.11, bf16[64,128]{1,0:T(8,128)(2,1)} %bitcast.9, bf16[16,32,512]{2,1,0:T(8,128)(2,1)} %gt.1), custom_call_target="tpu_custom_call" | custom-call | tf_op jit(solution)/shard_map/triangle_backward/pallas_call | solution.py:467
  99.6 0.0 copy-start
  99.6 2.3 %copy.10 = bf16[32,128,128]{2,1,0:T(8,128)(2,1)} copy(bf16[32,128,128]{2,1,0:T(8,128)(2,1)} %get-tuple-element.8) | data formatting | bytes 2097152
  102.0 0.0 copy-done
  102.0 0.6 copy.11
Async XLA Ops:
  99.6 2.3 %copy-start = (f32[64,128]{1,0:T(8,128)S(1)}, f32[64,128]{1,0:T(8,128)}, u32[]{:S(2)}) copy-start(f32[64,128]{1,0:T(8,128)} %get-tuple-element.5) | copy-start | bytes 98308

commit v4 on v3

--- a/solution.py
+++ b/solution.py
@@ -35,11 +35,11 @@
     nr, nc, nq,
     tok, pair_h, pm_h, gain_h, w_h, gt,
     out, wout,
-    tok_v, pair, pm, gain, w_v, mask, wt,
+    tok_v, pair, pm, gain, w_v, gq, mask, wt,
     normed, lt, rt, lrs, lrr, gfull, dsend, drecv, df, asend, arecv,
-    wf, fo, stdo, invo, gro, ag, wp, wr, zp, zq, zr, xr, wg,
+    wf, wfs, dno, fo, stdo, invo, gro, ag, wp, wr, zp, zq, zr, xr, wg,
     in_s, o_s,
-    g1_s, g1_r, g2_s, g2_r, wf_s, wf_r, lr_s, lr_r, d_s, d_r, a_s, a_r,
+    g1_s, g1_r, g2_s, g2_r, wf_s, wf_r, wx2_s, wx2_r, lr_s, lr_r, d_s, d_r, a_s, a_r,
     ag_s, ag_r, wa_s, wa_r, wx_s, wx_r, wz_s, wz_r, wb_s, wb_r, wd_s, wd_r,
 ):
     r = lax.axis_index("row")
@@ -51,6 +51,8 @@
     nj = gfull.shape[2]
     t_n = ni // nq
     jpb = nj // ni
+    gr_n = 4 // nr
+    wr_n = gr_n * hq
     npl = nc // 2
     nz = 2 * nq
     zh = lax.rem(lax.div(c, 2), 2)
@@ -78,6 +80,9 @@
     def to_z(i):
         return {"col": col_of(lax.div(i, nq), m), "ch": lax.rem(i, nq)}
 
+    lane = pl.ds(pl.multiple_of(r * nj, nj), nj)
+    mine = pltpu.make_async_copy(gt.at[:, :, lane], gq, in_s.at[5])
+    mine.start()
     loads = [
         pltpu.make_async_copy(src, dst, in_s.at[k])
         for k, (src, dst) in enumerate(
@@ -105,9 +110,6 @@
         greet({"col": col_of(1 - zh, m), "ch": lax.rem(q + off, nq)})
         return carry
     lax.fori_loop(1, nq, greet_far, 0)
-
-    for load in loads:
-        load.wait()
 
     def permuted(w):
         rows = []
@@ -126,21 +128,6 @@
                     at = g * hq + half * npl + y * 2
                     rows.append(w[at:at + 2])
         return jnp.concatenate(rows, axis=0)
-
-    wv = permuted(w_v[...].astype(F32)).astype(BF16)
-    wt[...] = wv
-    wf[q] = wv
-
-    tok_k = tok_v[pl.ds(r, 1), :]
-    first = c * ni
-    tok_i = tok_v[pl.ds(lax.div(first, nk), 1), :]
-    at = lax.broadcasted_iota(jnp.int32, (ni, nk), 1) - lax.rem(first, nk)
-    hit = at == lax.broadcasted_iota(jnp.int32, (ni, nk), 0)
-    tok_i = jnp.sum(jnp.where(hit, tok_i, 0).astype(F32), axis=1, keepdims=True)
-    mask[...] = (pm[...] * tok_k).astype(F32) * tok_i
-    gain_v = gain[...]
-
-    pl.semaphore_wait(barrier, nr + nc + 2 * nq - 4)
 
     def remote(src, dst, s, rr, device):
         return pltpu.make_async_remote_copy(
@@ -166,29 +153,41 @@
             return carry
         lax.fori_loop(1, size, one, 0)
 
-    lane = pl.ds(pl.multiple_of(r * nj, nj), nj)
 
     def rows_of(b):
         return pl.ds(pl.multiple_of(b * ni, ni), ni)
 
     def g1(to, src):
-        return remote(gt.at[to, :, lane], gfull.at[r, rows_of(src)],
+        return remote(gq.at[to], gfull.at[r, rows_of(src)],
                       g1_s.at[to], g1_r.at[src], to_col(to))
 
     def g2(to, src):
         return remote(gfull.at[src], gfull.at[src], g2_s.at[to], g2_r.at[src], to_row(to))
 
     def wfc(to, src):
-        return remote(wt, wf.at[src], wf_s.at[to], wf_r.at[src], to_ch(to))
-
-    def lrc(to, src):
-        return remote(lrs.at[pos(to)], lrr.at[src], lr_s.at[to], lr_r.at[src], to_col(to))
-
-    def dc(to, src):
-        return remote(dsend.at[to], drecv.at[src], d_s.at[to], d_r.at[src], to_plane(to))
-
-    def ac(to, src):
-        return remote(asend.at[to], arecv.at[src], a_s.at[to], a_r.at[src], to_z(to))
+        part = wt.at[pl.ds(pl.multiple_of(r * wr_n, wr_n), wr_n)]
+        return remote(part, wf.at[r, src], wf_s.at[to], wf_r.at[src], to_ch(to))
+
+    def wfx(to, src):
+        return remote(wf.at[src], wf.at[src], wx2_s.at[to], wx2_r.at[src], to_row(to))
+
+    def lrc(side):
+        def make(to, src):
+            return remote(lrs.at[side, pos(to)], lrr.at[side, src],
+                          lr_s.at[side, to], lr_r.at[side, src], to_col(to))
+        return make
+
+    def dc(side):
+        def make(to, src):
+            return remote(dsend.at[side, to], drecv.at[side, src],
+                          d_s.at[side, to], d_r.at[side, src], to_plane(to))
+        return make
+
+    def ac(side, u):
+        def make(to, src):
+            return remote(asend.at[side, u, to], arecv.at[side, u, src],
+                          a_s.at[side, u, to], a_r.at[side, u, src], to_z(to))
+        return make
 
     def wa(to, src):
         return remote(wp.at[to], wr.at[src], wa_s.at[to], wa_r.at[src], to_plane(to))
@@ -213,10 +212,26 @@
     def wd(to, src):
         return remote(wg.at[src], wg.at[src], wd_s.at[to], wd_r.at[src], to_plane(to))
 
+    pl.semaphore_wait(barrier, nr + nc + 2 * nq - 4)
+    mine.wait()
     spread(nc, c, g1)
+    for load in loads:
+        load.wait()
+    wv = permuted(w_v[...].astype(F32)).astype(BF16)
+    wt[...] = wv
+    wf[r, q] = wt[pl.ds(pl.multiple_of(r * wr_n, wr_n), wr_n), :]
+
+    tok_k = tok_v[pl.ds(r, 1), :]
+    first = c * ni
+    tok_i = tok_v[pl.ds(lax.div(first, nk), 1), :]
+    at = lax.broadcasted_iota(jnp.int32, (ni, nk), 1) - lax.rem(first, nk)
+    hit = at == lax.broadcasted_iota(jnp.int32, (ni, nk), 0)
+    tok_i = jnp.sum(jnp.where(hit, tok_i, 0).astype(F32), axis=1, keepdims=True)
+    mask[...] = (pm[...] * tok_k).astype(F32) * tok_i
+    gain_v = gain[...]
+
     spread(nq, q, wfc)
-    mine = pltpu.make_async_copy(gt.at[c, :, lane], gfull.at[r, rows_of(c)], g1_s.at[c])
-    mine.start()
+    gfull[r, rows_of(c)] = gq[c]
 
     def mask_of(i):
         return mask[pl.ds(i, 1), :]
@@ -234,17 +249,18 @@
 
     lax.fori_loop(0, ni, project, 0, unroll=4)
 
-    for h in range(hq):
-        lrs[h, 0] = lt[:, h, :].astype(BF16)
-        lrs[h, 1] = rt[:, h, :].astype(BF16)
-    spread(nc, c, lrc)
-    lrr[c] = lrs[pos(c)]
+    for side, made in ((0, lt), (1, rt)):
+        for h in range(hq):
+            lrs[side, h] = made[:, h, :].astype(BF16)
+        spread(nc, c, lrc(side))
+        lrr[side, c] = lrs[side, pos(c)]
 
     gather(nc, c, g1)
-    mine.wait()
     spread(nr, r, g2)
 
     gather(nq, q, wfc)
+    spread(nr, r, wfx)
+    gather(nr, r, wfx)
 
     def own(t, carry):
         i = q * t_n + t
@@ -253,46 +269,83 @@
         invo[t] = jnp.broadcast_to(inv, (nk, cc))
         p = lax.dot_general(wf[...].reshape(nq * 4 * hq, cc), normed[i], NT,
                             preferred_element_type=F32)
-        p = p.reshape(nq, 4, hq, nk)
-        f = factors((p[:, 0], p[:, 1], p[:, 2], p[:, 3]), mask_of(i))
+        p = p.reshape(nr, nq, gr_n, hq, nk)
+        f = factors(tuple(p[g // gr_n, :, g % gr_n] for g in range(4)), mask_of(i))
         for g in range(4):
             fo[t, g] = f[g]
         return carry
 
-    lax.fori_loop(0, t_n, own, 0)
-
+    tu = t_n // 2
+
+    def return_side(side, d):
+        for cb in range(nc):
+            dsend[side, cb // 4 * 2 + cb % 2, cb // 2 % 2] = d[cb]
+        spread(npl, m, dc(side))
+        drecv[side, m] = dsend[side, m]
+
+    def forward_side(side):
+        gather(npl, m, dc(side))
+        for half in range(2):
+            df[half] = drecv[side, :, half].astype(F32)
+        for u in range(tu):
+            for half in range(2):
+                for b in range(nq):
+                    i = b * t_n + 2 * u
+                    asend[side, u, half * nq + b] = jnp.concatenate(
+                        [df[half, :, i, :], df[half, :, i + 1, :]], axis=0).astype(BF16)
+            spread(nz, z, ac(side, u))
+            arecv[side, u, z] = asend[side, u, z]
+
+    lax.fori_loop(0, tu, own, 0)
     gather(nr, r, g2)
-    gather(nc, c, lrc)
-
-    left_all = lrr[:, 0].reshape(n, nk)
+    gather(nc, c, lrc(0))
+    left_all = lrr[0].reshape(n, nk)
+    dr = []
+    for x in range(nr):
+        d = lax.dot_general(gfull[x], left_all, TN, preferred_element_type=F32)
+        dr.append(d.astype(BF16).reshape(jpb, ni, nk))
+    return_side(1, [dr[cb // jpb][cb % jpb] for cb in range(nc)])
+    lax.fori_loop(tu, t_n, own, 0)
+    for side in range(2):
+        for b in range(nq):
+            for gg in range(2):
+                g, row = side * 2 + gg, (b * 2 + gg) * hq
+                at = g % gr_n * hq
+                wfs[side, row:row + hq] = wf[g // gr_n, b, at:at + hq]
+    forward_side(1)
+
+    gather(nc, c, lrc(1))
     dl = jnp.zeros((n, nk), F32)
     for x in range(nr):
-        rx = lrr[x * jpb:(x + 1) * jpb, 1].reshape(nj, nk)
+        rx = lrr[1, x * jpb:(x + 1) * jpb].reshape(nj, nk)
         dl = dl + jnp.dot(gfull[x], rx, preferred_element_type=F32)
-        dr = lax.dot_general(gfull[x], left_all, TN, preferred_element_type=F32)
-        dr = dr.astype(BF16).reshape(jpb, ni, nk)
-        for b in range(jpb):
-            cb = x * jpb + b
-            dsend[cb // 4 * 2 + cb % 2, cb // 2 % 2, 1] = dr[b]
     dl = dl.astype(BF16).reshape(nc, ni, nk)
-    for cb in range(nc):
-        dsend[cb // 4 * 2 + cb % 2, cb // 2 % 2, 0] = dl[cb]
-    spread(npl, m, dc)
-    drecv[m] = dsend[m]
-    gather(npl, m, dc)
-
-    for half in range(2):
-        for side in range(2):
-            df[half, side] = drecv[:, half, side].astype(F32)
-    for half in range(2):
-        for b in range(nq):
-            for t in range(t_n):
-                i = b * t_n + t
-                asend[half * nq + b, t] = jnp.concatenate(
-                    [df[half, 0, :, i, :], df[half, 1, :, i, :]], axis=0).astype(BF16)
-    spread(nz, z, ac)
-    arecv[z] = asend[z]
-    gather(nz, z, ac)
+    return_side(0, [dl[cb] for cb in range(nc)])
+    forward_side(0)
+
+    def side_grads(side, t):
+        u, at = t // 2, t % 2 * npl
+        d = jnp.stack([
+            jnp.stack([arecv[side, u, half * nq + b].astype(F32)[at:at + npl]
+                       for half in range(2)])
+            for b in range(nq)]).reshape(nq, hq, nk)
+        gr = jnp.stack([d * fo[t, 2 * side], d * fo[t, 2 * side + 1]], axis=1)
+        gr = gr.reshape(nq * 2 * hq, nk).astype(BF16)
+        gro[side, :, t * nk:(t + 1) * nk] = gr
+        return lax.dot_general(gr, wfs[side], TN, preferred_element_type=F32)
+
+    def w_side(side):
+        nb = normed[pl.ds(q * t_n, t_n)].reshape(t_n * nk, cc)
+        part = jnp.dot(gro[side], nb, preferred_element_type=F32)
+        part = part.reshape(nq, npl // 2, 8, cc)
+        for b in range(npl // 2):
+            wp[side * (npl // 2) + b] = part[:, b]
+
+    for u in range(tu):
+        gather(nz, z, ac(1, u))
+    for t in range(t_n):
+        dno[t] = side_grads(1, t)
+    w_side(1)
 
     def to_right(b, t):
         return remote(ag.at[b, t], ag.at[b, t], ag_s.at[0, b, t], ag_r.at[b, t],
@@ -305,19 +358,35 @@
     def keep(b, t):
         return pltpu.make_async_copy(ag.at[b, t], out.at[b * t_n + t], o_s.at[b, t])
 
+    def relay_one(s, t):
+        @pl.when(q >= s)
+        def _():
+            to_right(q - s, t).wait_recv()
+
+            @pl.when(q < nq - 1)
+            def _():
+                to_right(q - s, t).start()
+            keep(q - s, t).start()
+
+        @pl.when(q + s < nq)
+        def _():
+            to_left(q + s, t).wait_recv()
+
+            @pl.when(q > 0)
+            def _():
+                to_left(q + s, t).start()
+            keep(q + s, t).start()
+
+    def relay(s):
+        def one(t, carry):
+            relay_one(s, t)
+            return carry
+        lax.fori_loop(0, t_n, one, 0)
+
     for t in range(t_n):
-        d = jnp.stack([
-            jnp.stack([arecv[half * nq + b, t].astype(F32) for half in range(2)])
-            for b in range(nq)])
-        d0 = d[:, :, :npl].reshape(nq, hq, nk)
-        d1 = d[:, :, npl:].reshape(nq, hq, nk)
-        f = fo[t]
-        gr = jnp.stack([d0 * f[0], d0 * f[1], d1 * f[2], d1 * f[3]], axis=1)
-        gr = gr.reshape(nq * 4 * hq, nk).astype(BF16)
-        gro[:, t * nk:(t + 1) * nk] = gr
-        d_norm = lax.dot_general(gr, wf[...].reshape(nq * 4 * hq, cc),
-                                 TN, preferred_element_type=F32)
-        e = d_norm * gain_v
+        if t % 2 == 0:
+            gather(nz, z, ac(0, t // 2))
+        e = (side_grads(0, t) + dno[t]) * gain_v
         std = stdo[t]
         first = jnp.mean(e, axis=-1, keepdims=True)
         second = jnp.mean(e * std, axis=-1, keepdims=True)
@@ -332,33 +401,8 @@
         def _():
             to_left(q, t).start()
 
-    def relay(s):
-        def one(t, carry):
-            @pl.when(q >= s)
-            def _():
-                to_right(q - s, t).wait_recv()
-
-                @pl.when(q < nq - 1)
-                def _():
-                    to_right(q - s, t).start()
-                keep(q - s, t).start()
-
-            @pl.when(q + s < nq)
-            def _():
-                to_left(q + s, t).wait_recv()
-
-                @pl.when(q > 0)
-                def _():
-                    to_left(q + s, t).start()
-                keep(q + s, t).start()
-            return carry
-        lax.fori_loop(0, t_n, one, 0)
-
     def w_own():
-        nb = normed[pl.ds(q * t_n, t_n)].reshape(t_n * nk, cc)
-        w_part = jnp.dot(gro[...], nb, preferred_element_type=F32).reshape(nq, npl, 8, cc)
-        for b in range(npl):
-            wp[b] = w_part[:, b]
+        w_side(0)
         spread(npl, m, wa)
         wr[m] = wp[m]
 
@@ -418,10 +462,14 @@
 
     spread(nc, c, g1, False)
     spread(nq, q, wfc, False)
-    spread(nc, c, lrc, False)
+    spread(nr, r, wfx, False)
+    for side in range(2):
+        spread(nc, c, lrc(side), False)
     spread(nr, r, g2, False)
-    spread(npl, m, dc, False)
-    spread(nz, z, ac, False)
+    for side in range(2):
+        spread(npl, m, dc(side), False)
+        for u in range(tu):
+            spread(nz, z, ac(side, u), False)
     spread(npl, m, wa, False)
     spread(nr, r, wx, False)
     for half in range(2):
@@ -478,24 +526,27 @@
             pltpu.VMEM((ni, nk), jnp.int32),
             pltpu.VMEM((1, cc), F32),
             pltpu.VMEM((4 * hq, cc), BF16),
+            pltpu.VMEM((nc, ni, nj), BF16),
             pltpu.VMEM((ni, nk), F32),
             pltpu.VMEM((4 * hq, cc), BF16),
             pltpu.VMEM((ni, nk, cc), BF16),
             pltpu.VMEM((ni, hq, nk), F32),
             pltpu.VMEM((ni, hq, nk), F32),
-            pltpu.VMEM((nc, 2, ni, nk), BF16),
-            pltpu.VMEM((nc, 2, ni, nk), BF16),
+            pltpu.VMEM((2, nc, ni, nk), BF16),
+            pltpu.VMEM((2, nc, ni, nk), BF16),
             pltpu.VMEM((nr, n, nj), BF16),
-            pltpu.VMEM((npl, 2, 2, ni, nk), BF16),
-            pltpu.VMEM((npl, 2, 2, ni, nk), BF16),
-            pltpu.VMEM((2, 2, npl, ni, nk), F32),
-            pltpu.VMEM((nz, t_n, hq, nk), BF16),
-            pltpu.VMEM((nz, t_n, hq, nk), BF16),
-            pltpu.VMEM((nq, 4 * hq, cc), BF16),
+            pltpu.VMEM((2, npl, 2, ni, nk), BF16),
+            pltpu.VMEM((2, npl, 2, ni, nk), BF16),
+            pltpu.VMEM((2, npl, ni, nk), F32),
+            pltpu.VMEM((2, t_n // 2, nz, hq, nk), BF16),
+            pltpu.VMEM((2, t_n // 2, nz, hq, nk), BF16),
+            pltpu.VMEM((nr, nq, 4 // nr * hq, cc), BF16),
+            pltpu.VMEM((2, nq * 2 * hq, cc), BF16),
+            pltpu.VMEM((t_n, nk, cc), F32),
             pltpu.VMEM((t_n, 4, nq, hq, nk), F32),
             pltpu.VMEM((t_n, nk, cc), F32),
             pltpu.VMEM((t_n, nk, cc), F32),
-            pltpu.VMEM((nq * 4 * hq, t_n * nk), BF16),
+            pltpu.VMEM((2, nq * 2 * hq, t_n * nk), BF16),
             pltpu.VMEM((nq, t_n, nk, cc), BF16),
             pltpu.VMEM((npl, nq, 8, cc), F32),
             pltpu.VMEM((npl, nq, 8, cc), F32),
@@ -504,9 +555,10 @@
             pltpu.VMEM((nz, 8, cc), F32),
             pltpu.VMEM((nr, nq // nr, 8, cc), F32),
             pltpu.VMEM((npl, 8, cc), F32),
-            dma(5), dma(nq, t_n),
-            dma(nc), dma(nc), dma(nr), dma(nr), dma(nq), dma(nq),
-            dma(nc), dma(nc), dma(npl), dma(npl), dma(nz), dma(nz),
+            dma(6), dma(nq, t_n),
+            dma(nc), dma(nc), dma(nr), dma(nr), dma(nq), dma(nq), dma(nr), dma(nr),
+            dma(2, nc), dma(2, nc), dma(2, npl), dma(2, npl),
+            dma(2, t_n // 2, nz), dma(2, t_n // 2, nz),
             dma(2, nq, t_n), dma(nq, t_n),
             dma(npl), dma(npl), dma(nr), dma(nr), dma(2, nq // nr), dma(nz), dma(nr), dma(1),
             dma(npl), dma(npl),

time: 103 us -> 100 us (0.971)
  Pallas kernels: 99 us -> 95.4 us
    pallas_call x1, Pallas kernels: 99 us -> 95.4 us  [body(): pl.pallas_call(functools.partial(kernel, nr, nc, nq), out_shape=(jax.Shap...]
where the time goes in v4:
time: 100 us; the launch traced here: 99 us
  Pallas kernels  95.4 us (95%)
  local copies, waits for them, and re-layouts  2.93 us (3%)
    pallas_call x1, Pallas kernels, body(): pl.pallas_call(functools.partial(kernel, nr, nc, nq), out_shape=(jax.Shap...  95.4 us
    unnamed x4, local copies, waits for them, and re-layouts  2.93 us

profile of v4, /device:TPU:1, one launch (start us, length us, event | category | flops | bytes accessed | tf_op | source)
XLA Modules:
  0.0 99.0 jit_solution(12618134685912373671)
XLA Ops:
  0.6 95.4 %triangle_backward.1 = (bf16[32,128,128]{2,1,0:T(8,128)(2,1)}, f32[64,128]{1,0:T(8,128)}) custom-call(s32[4,128]{1,0:T(4,128)} %bitcast.10, bf16[32,128,128]{2,1,0:T(8,128)(2,1)} %pair_h.1, s32[32,128]{1,0:T(8,128)} %pm_h.1, f32[1,128]{1,0:T(1,128)} %bitcast.11, bf16[64,128]{1,0:T(8,128)(2,1)} %bitcast.9, bf16[16,32,512]{2,1,0:T(8,128)(2,1)} %gt.1), custom_call_target="tpu_custom_call" | custom-call | tf_op jit(solution)/shard_map/triangle_backward/pallas_call | solution.py:515
  96.1 0.0 copy-start
  96.1 2.3 %copy.10 = bf16[32,128,128]{2,1,0:T(8,128)(2,1)} copy(bf16[32,128,128]{2,1,0:T(8,128)(2,1)} %get-tuple-element.8) | data formatting | bytes 2097152
  98.4 0.0 copy-done
  98.4 0.6 copy.11
Async XLA Ops:
  96.1 2.3 %copy-start = (f32[64,128]{1,0:T(8,128)S(1)}, f32[64,128]{1,0:T(8,128)}, u32[]{:S(2)}) copy-start(f32[64,128]{1,0:T(8,128)} %get-tuple-element.5) | copy-start | bytes 98308

commit v5 on v4

--- a/solution.py
+++ b/solution.py
@@ -446,10 +446,11 @@
     def w_last():
         gather(npl, m, wd)
 
-    steps = {1: [w_own], 2: [w_plane], 3: [w_rows], 5: [w_ring], 6: [w_share]}
+    steps = {0: [w_own], 1: [w_plane], 2: [w_rows], 4: [w_ring], 5: [w_share]}
     done = set()
-    for s in range(1, nq):
-        relay(s)
+    for s in range(nq):
+        if s > 0:
+            relay(s)
         for step in steps.get(s, ()):
             step()
             done.add(step)

time: 100 us -> 97.3 us (0.973)
  Pallas kernels: 95.4 us -> 92.3 us
    pallas_call x1, Pallas kernels: 95.4 us -> 92.3 us  [body(): pl.pallas_call(functools.partial(kernel, nr, nc, nq), out_shape=(jax.Shap...]
where the time goes in v5:
time: 97.3 us; the launch traced here: 95.9 us
  Pallas kernels  92.3 us (95%)
  local copies, waits for them, and re-layouts  2.93 us (3%)
    pallas_call x1, Pallas kernels, body(): pl.pallas_call(functools.partial(kernel, nr, nc, nq), out_shape=(jax.Shap...  92.3 us
    unnamed x4, local copies, waits for them, and re-layouts  2.93 us

profile of v5, /device:TPU:1, one launch (start us, length us, event | category | flops | bytes accessed | tf_op | source)
XLA Modules:
  0.0 95.9 jit_solution(15306922381005876023)
XLA Ops:
  0.6 92.3 %triangle_backward.1 = (bf16[32,128,128]{2,1,0:T(8,128)(2,1)}, f32[64,128]{1,0:T(8,128)}) custom-call(s32[4,128]{1,0:T(4,128)} %bitcast.10, bf16[32,128,128]{2,1,0:T(8,128)(2,1)} %pair_h.1, s32[32,128]{1,0:T(8,128)} %pm_h.1, f32[1,128]{1,0:T(1,128)} %bitcast.11, bf16[64,128]{1,0:T(8,128)(2,1)} %bitcast.9, bf16[16,32,512]{2,1,0:T(8,128)(2,1)} %gt.1), custom_call_target="tpu_custom_call" | custom-call | tf_op jit(solution)/shard_map/triangle_backward/pallas_call | solution.py:516
  93.0 0.0 copy-start
  93.0 2.3 %copy.10 = bf16[32,128,128]{2,1,0:T(8,128)(2,1)} copy(bf16[32,128,128]{2,1,0:T(8,128)(2,1)} %get-tuple-element.8) | data formatting | bytes 2097152
  95.3 0.0 copy-done
  95.3 0.6 copy.11
Async XLA Ops:
  93.0 2.3 %copy-start = (f32[64,128]{1,0:T(8,128)S(1)}, f32[64,128]{1,0:T(8,128)}, u32[]{:S(2)}) copy-start(f32[64,128]{1,0:T(8,128)} %get-tuple-element.5) | copy-start | bytes 98308

commit v6 on v5

--- a/solution.py
+++ b/solution.py
@@ -446,7 +446,7 @@
     def w_last():
         gather(npl, m, wd)
 
-    steps = {0: [w_own], 1: [w_plane], 2: [w_rows], 4: [w_ring], 5: [w_share]}
+    steps = {0: [w_own], 1: [w_plane], 2: [w_rows], 3: [w_ring], 4: [w_share]}
     done = set()
     for s in range(nq):
         if s > 0:

time: 97.3 us -> 100 us (1.028)
  Pallas kernels: 92.3 us -> 95.4 us
    pallas_call x1, Pallas kernels: 92.3 us -> 95.4 us  [body(): pl.pallas_call(functools.partial(kernel, nr, nc, nq), out_shape=(jax.Shap...]
where the time goes in v6:
time: 100 us; the launch traced here: 99 us
  Pallas kernels  95.4 us (95%)
  local copies, waits for them, and re-layouts  2.93 us (3%)
    pallas_call x1, Pallas kernels, body(): pl.pallas_call(functools.partial(kernel, nr, nc, nq), out_shape=(jax.Shap...  95.4 us
    unnamed x4, local copies, waits for them, and re-layouts  2.93 us

profile of v6, /device:TPU:1, one launch (start us, length us, event | category | flops | bytes accessed | tf_op | source)
XLA Modules:
  0.0 99.0 jit_solution(15652880433697174797)
XLA Ops:
  0.6 95.4 %triangle_backward.1 = (bf16[32,128,128]{2,1,0:T(8,128)(2,1)}, f32[64,128]{1,0:T(8,128)}) custom-call(s32[4,128]{1,0:T(4,128)} %bitcast.10, bf16[32,128,128]{2,1,0:T(8,128)(2,1)} %pair_h.1, s32[32,128]{1,0:T(8,128)} %pm_h.1, f32[1,128]{1,0:T(1,128)} %bitcast.11, bf16[64,128]{1,0:T(8,128)(2,1)} %bitcast.9, bf16[16,32,512]{2,1,0:T(8,128)(2,1)} %gt.1), custom_call_target="tpu_custom_call" | custom-call | tf_op jit(solution)/shard_map/triangle_backward/pallas_call | solution.py:516
  96.0 0.0 copy-start
  96.1 2.3 %copy.10 = bf16[32,128,128]{2,1,0:T(8,128)(2,1)} copy(bf16[32,128,128]{2,1,0:T(8,128)(2,1)} %get-tuple-element.8) | data formatting | bytes 2097152
  98.4 0.0 copy-done
  98.4 0.6 copy.11
Async XLA Ops:
  96.0 2.3 %copy-start = (f32[64,128]{1,0:T(8,128)S(1)}, f32[64,128]{1,0:T(8,128)}, u32[]{:S(2)}) copy-start(f32[64,128]{1,0:T(8,128)} %get-tuple-element.5) | copy-start | bytes 98308
